TPU v7x, 32 devices: a whole 2x2x4 slice. The times are simulated.
32 devices in a mesh: date: 4 (over y, core), tile: 8 (over z, x).
Axes of the slice: x: 2, y: 2, z: 4, core: 2. Of those that a mesh axis runs over, the one named last changes fastest.
Arguments:
- granules: bfloat16 [16, 10, 640, 512], P('date', None, 'tile'), may hold values from -6 to 6
- coef_x: bfloat16 [8, 5, 128, 12], P('tile'), may hold values from -1.75 to 1.75
- coef_y: bfloat16 [8, 5, 16, 12], P('tile'), may hold values from -1.75 to 1.75
- row_offset: int32 [8, 5], P('tile'), may hold values from 0 to 36
- col_offset: int32 [8, 5], P('tile'), may hold values from 0 to 244
- targets: int32 [8, 5], P('tile'), may hold values from -1 to 7, as said below
- mask: int32 [16, 8], P(None, 'tile'), may hold values from 0 to 1, as said below
- smoother: float32 [16, 16], replicated, as said below
Outputs:
- smoothed: float32 [16, 10, 8, 2048], P(None, None, 'tile', 'date')
Inputs may be any that keep to these rules, and one draw needn't show every extreme that they name: `targets`: slot 0 of granule g names tile g; the other slots name, in an order drawn from the seed, each tile other than g within 2 of g in index once, and -1 where such a tile lies beyond the ends. `mask`: every tile has at least one valid date. `smoother`: every entry is positive.
All inputs are finite; a program needn't handle non-finite values.
Results may differ from a plain program's by a relative error of at most 0.0004.
Values sent between devices are 32-bit elements; how exact they have to be, the bound alone decides.
A program may use at most 128 MiB of HBM per device.

v0:
```python
import jax
import jax.numpy as jnp
from jax import lax
from jax.sharding import PartitionSpec as P

RADIUS = 2


def shifted(block, axis, distance):
    devices = range(lax.axis_size(axis))
    route = [(i - distance, i) for i in devices if i - distance in devices]
    return lax.ppermute(block, axis, route)


def band_matrix(coeffs, offset, span_width):
    row_count = coeffs.shape[0]
    row_ids = jnp.arange(row_count, dtype=jnp.int32)[:, None]
    col_ids = jnp.arange(span_width, dtype=jnp.int32)[None, :]
    tap_index = col_ids - 2 * row_ids - offset
    banded = jnp.zeros((row_count, span_width), jnp.float32)
    for tap_number in range(coeffs.shape[1]):
        picked = coeffs[:, tap_number : tap_number + 1].astype(jnp.float32)
        banded = banded + jnp.where(tap_index == tap_number, picked, jnp.float32(0.0))
    return banded


def body(granules, coef_x, coef_y, row_offset, col_offset, targets, mask, smoother):
    local_dates, band_count, grid_rows, grid_cols = granules.shape
    slot_count = coef_x.shape[1]
    tile_cols = coef_x.shape[2]
    tile_rows = coef_y.shape[2]
    x_mats = jnp.concatenate(
        [
            band_matrix(coef_x[0, slot], col_offset[0, slot], grid_cols)
            for slot in range(slot_count)
        ],
        0,
    ).astype(jnp.bfloat16)
    x_pass = jnp.dot(granules.reshape(-1, grid_cols), x_mats.T, preferred_element_type=jnp.float32)
    x_pass = x_pass.reshape(local_dates, band_count, grid_rows, slot_count, tile_cols)
    y_mats = jnp.stack(
        [
            band_matrix(coef_y[0, slot], row_offset[0, slot], grid_rows)
            for slot in range(slot_count)
        ],
        0,
    )
    partials = jnp.einsum("kir,dbrkj->kdbij", y_mats, x_pass, precision=lax.Precision.HIGHEST)
    flat_parts = partials.reshape(slot_count, -1)
    aimed = targets[0]
    own_tile = lax.axis_index("tile")

    def aimed_at(reach):
        chosen = (aimed == own_tile + reach).astype(jnp.float32)
        return jnp.dot(chosen, flat_parts, precision=lax.Precision.HIGHEST)

    tiled = aimed_at(0)
    for reach in [step for step in range(-RADIUS, RADIUS + 1) if step != 0]:
        tiled = tiled + shifted(aimed_at(reach), "tile", reach)
    series = tiled.reshape(local_dates, band_count, tile_rows * tile_cols)
    all_dates = smoother.shape[0]
    block_pix = tile_rows * tile_cols // lax.axis_size("date")
    weight = mask[:, 0].astype(jnp.float32)
    denominator = jnp.dot(smoother, weight, precision=lax.Precision.HIGHEST)
    gathered = lax.all_to_all(series, "date", split_axis=2, concat_axis=0, tiled=True)
    weighted = gathered * weight[:, None, None]
    numerator = jnp.einsum("ts,sbp->tbp", smoother, weighted, precision=lax.Precision.HIGHEST)
    smoothed = numerator / denominator[:, None, None]
    return smoothed.reshape(all_dates, band_count, 1, block_pix)


def solution(mesh):
    return jax.shard_map(
        body,
        mesh=mesh,
        in_specs=(
            P("date", None, "tile", None),
            P("tile", None, None, None),
            P("tile", None, None, None),
            P("tile", None),
            P("tile", None),
            P("tile", None),
            P(None, "tile"),
            P(),
        ),
        out_specs=P(None, None, "tile", "date"),
        check_vma=False,
    )
```

profile of v0, /device:TPU:24, one launch (start us, length us, event | category | flops | bytes accessed | tf_op | source)
XLA Modules:
  0.0 145.7 jit_solution(1445991004848718412)
XLA Ops:
  0.0 0.9 slice_bitcast_fusion.5
  0.9 1.5 %fusion.234 = (s32[1,1]{1,0:T(1,128)}, s32[1,1]{1,0:T(1,128)}, s32[1,1]{1,0:T(1,128)}, s32[1,1]{1,0:T(1,128)}, s32[1,1]{1,0:T(1,128)}) fusion(s32[1,5]{1,0:T(1,128)} %param.12), kind=kLoop, calls=%fused_computation.383 | loop fusion | bytes 40 | tf_op jit(solution)/shard_map/slice | solution.py:34
  2.5 1.0 fusion.85
  3.5 0.9 fusion.86
  4.5 1.1 fusion.87
  5.6 1.0 fusion.88
  6.6 1.0 fusion.89
  7.6 5.6 %convolution_bitcast_fusion = f32[3200,640]{0,1:T(8,128)} fusion(bf16[640,512]{1,0:T(8,128)(2,1)S(1)} %fusion.89, bf16[3200,512]{1,0:T(8,128)(2,1)S(1)} %bitcast.401), kind=kOutput, calls=%fused_computation.2 | convolution fusion | flops 2097152000 | bytes 12124160 | tf_op jit(solution)/shard_map/dot_general | solution.py:39
  13.3 17.5 %reshape.2577 = f32[4,10,80,5,128]{2,1,0,4,3:T(8,128)} reshape(f32[3200,640]{0,1:T(8,128)} %convolution_bitcast_fusion) | data formatting | bytes 16384000 | tf_op jit(solution)/shard_map/reshape | solution.py:40
  30.8 0.3 convert_reduce_fusion.59
  31.1 0.7 fusion.233
  31.7 0.3 convert_reduce_fusion.47
  32.0 0.3 convert_reduce_fusion.35
  32.2 0.3 convert_reduce_fusion.23
  32.5 0.3 convert_reduce_fusion.11
  32.8 0.7 constant_dynamic-update-slice_fusion.4
  33.4 0.7 constant_dynamic-update-slice_fusion.3
  34.1 0.7 constant_dynamic-update-slice_fusion.2
  34.9 0.8 constant_dynamic-update-slice_fusion.1
  35.6 0.7 constant_dynamic-update-slice_fusion
  36.4 0.0 copy-start.4
  36.4 24.8 %fusion = f32[5,4,10,128,16]{3,4,2,1,0:T(8,128)} fusion(f32[4,10,80,5,128]{2,1,0,4,3:T(8,128)} %reshape.2577, f32[5,16,80]{2,1,0:T(8,128)S(1)} %constant_dynamic-update-slice_fusion), kind=kOutput, calls=%fused_computation | convolution fusion | flops 393216000 | bytes 9856000 | tf_op jit(solution)/shard_map/kir,dbrkj->kdbij/dot_general | solution.py:48
  61.2 4.3 %fusion.8 = f32[1,81920]{1,0:T(1,128)} fusion(f32[1,5,640,128]{3,2,1,0:T(8,128)} %bitcast.402, s32[1,5]{1,0:T(1,128)S(1)} %copy-done.4, s32[]{:T(128)S(6)} %add.849), kind=kOutput, calls=%fused_computation.9 | convolution fusion | flops 4915205 | bytes 1966104 | tf_op jit(solution)/shard_map/dot_general | solution.py:55
  65.6 3.1 %collective-permute-start = (f32[81920]{0:T(1024)}, f32[81920]{0:T(1024)}, u32[]{:S(2)}, u32[]{:S(2)}) collective-permute-start(f32[81920]{0:T(1024)} %bitcast.90), channel_id=1, source_target_pairs={{2,0},{3,1},{4,2},{5,3},{6,4},{7,5},{10,8},{11,9},{12,10},{13,11},... | collective-permute-start | bytes 983048 | tf_op jit(solution)/shard_map/ppermute | solution.py:12
  68.6 4.3 %fusion.6 = f32[1,81920]{1,0:T(1,128)} fusion(f32[1,5,640,128]{3,2,1,0:T(8,128)} %bitcast.403, s32[1,5]{1,0:T(1,128)S(1)} %copy-done.4, s32[]{:T(128)S(6)} %add.851), kind=kOutput, calls=%fused_computation.7 | convolution fusion | flops 4915205 | bytes 1966104 | tf_op jit(solution)/shard_map/dot_general | solution.py:55
  73.0 2.6 %collective-permute-start.1 = (f32[81920]{0:T(1024)}, f32[81920]{0:T(1024)}, u32[]{:S(2)}, u32[]{:S(2)}) collective-permute-start(f32[81920]{0:T(1024)} %bitcast.93), channel_id=1, source_target_pairs={{1,0},{2,1},{3,2},{4,3},{5,4},{6,5},{7,6},{9,8},{10,9},{11,10},{12... | collective-permute-start | bytes 983048 | tf_op jit(solution)/shard_map/ppermute | solution.py:12
  75.5 4.3 %fusion.4 = f32[1,81920]{1,0:T(1,128)} fusion(f32[1,5,640,128]{3,2,1,0:T(8,128)} %bitcast.404, s32[1,5]{1,0:T(1,128)S(1)} %copy-done.4, s32[]{:T(128)S(6)} %add.853), kind=kOutput, calls=%fused_computation.5 | convolution fusion | flops 4915205 | bytes 1966104 | tf_op jit(solution)/shard_map/dot_general | solution.py:55
  79.9 4.0 %collective-permute-start.2 = (f32[81920]{0:T(1024)}, f32[81920]{0:T(1024)}, u32[]{:S(2)}, u32[]{:S(2)}) collective-permute-start(f32[81920]{0:T(1024)} %bitcast.96), channel_id=1, source_target_pairs={{0,1},{1,2},{2,3},{3,4},{4,5},{5,6},{6,7},{8,9},{9,10},{10,11},{11... | collective-permute-start | bytes 983048 | tf_op jit(solution)/shard_map/ppermute | solution.py:12
  83.9 3.7 %fusion.2 = f32[1,81920]{1,0:T(1,128)S(1)} fusion(f32[1,5,640,128]{3,2,1,0:T(8,128)} %bitcast.405, s32[1,5]{1,0:T(1,128)S(1)} %copy-done.4, s32[]{:T(128)S(6)} %add.855), kind=kOutput, calls=%fused_computation.3 | convolution fusion | flops 4915205 | bytes 1966104 | tf_op jit(solution)/shard_map/dot_general | solution.py:55
  87.6 1.3 collective-permute-start.3
  88.9 2.2 %fusion.10 = f32[1,81920]{1,0:T(1,128)S(1)} fusion(f32[1,5,640,128]{3,2,1,0:T(8,128)S(1)} %bitcast.406, s32[1,5]{1,0:T(1,128)S(1)} %copy-done.4, s32[]{:T(128)S(6)} %axis_index.12), kind=kOutput, calls=%fused_computation.11 | convolution fusion | flops 4915205 | bytes 1966104 | tf_op jit(solution)/shard_map/dot_general | solution.py:55
  91.1 0.0 collective-permute-done.1
  91.1 2.2 %collective-permute-done.2 = f32[81920]{0:T(1024)} collective-permute-done((f32[81920]{0:T(1024)}, f32[81920]{0:T(1024)}, u32[]{:S(2)}, u32[]{:S(2)}) %collective-permute-start.2) | collective-permute-done | bytes 327712 | tf_op jit(solution)/shard_map/ppermute | solution.py:12
  93.3 4.7 %collective-permute-done.3 = f32[81920]{0:T(1024)S(1)} collective-permute-done((f32[81920]{0:T(1024)S(1)}, f32[81920]{0:T(1024)S(1)}, u32[]{:S(2)}, u32[]{:S(2)}) %collective-permute-start.3) | collective-permute-done | bytes 327712 | tf_op jit(solution)/shard_map/ppermute | solution.py:12
  98.1 2.0 %add_add_fusion = f32[81920]{0:T(1024)} fusion(f32[81920]{0:T(1024)S(1)} %collective-permute-done.3, f32[81920]{0:T(1024)} %collective-permute-done.2, f32[81920]{0:T(1024)} %collective-permute-done.1, f32[81920]{0:T(1024)S(1)} %bitcast.409, f32[81920]{0:T(1024)} %collective-permute-done), kind=kLoop, calls=%fused_computation.22 | loop fusion | flops 327680 | bytes 1966080 | tf_op jit(solution)/shard_map/add | solution.py:59
  100.1 1.8 %reshape.2441 = f32[4,10,2048]{2,1,0:T(8,128)} reshape(f32[81920]{0:T(1024)} %add_add_fusion) | data formatting | bytes 655360 | tf_op jit(solution)/shard_map/reshape | solution.py:60
  101.9 4.5 %copy.22 = f32[4,10,2048]{1,0,2:T(4,128)} copy(f32[4,10,2048]{2,1,0:T(8,128)} %reshape.2441) | data formatting | bytes 655360 | tf_op jit(solution)/shard_map/reshape | solution.py:60
  106.4 7.3 %reshape.2638 = f32[4,1,20480]{2,1,0:T(1,128)} reshape(f32[2048,4,10]{2,1,0:T(4,128)} %bitcast.407) | data formatting | bytes 655360
  113.7 4.1 %all-to-all-start = ((f32[4,1,20480]{2,1,0:T(1,128)}), f32[4,1,20480]{2,1,0:T(1,128)}, u32[]{:S(2)}, u32[]{:S(2)}) async-start(f32[4,1,20480]{2,1,0:T(1,128)} %reshape.2638), calls=%async_computation | async-start | bytes 655360 | tf_op jit(solution)/shard_map/all_to_all | solution.py:65
  117.8 0.1 convolution_bitcast_fusion.1
  118.0 6.6 %all-to-all-done = f32[4,1,20480]{2,1,0:T(1,128)} async-done(((f32[4,1,20480]{2,1,0:T(1,128)}), f32[4,1,20480]{2,1,0:T(1,128)}, u32[]{:S(2)}, u32[]{:S(2)}) %all-to-all-start) | async-done | bytes 327712 | tf_op jit(solution)/shard_map/all_to_all | solution.py:65
  124.6 0.6 broadcast.2156
  125.2 3.2 %reduce.120 = f32[4,20480]{1,0:T(4,128)} reduce(f32[4,1,20480]{2,1,0:T(1,128)} %all-to-all-done, f32[]{:T(128)} %broadcast.2156), dimensions={1}, to_apply=%all_to_all.13.reduce_sub_computation | reduce | bytes 655364 | tf_op jit(solution)/shard_map/all_to_all | solution.py:65
  128.4 8.5 %reshape.2639 = f32[2048,4,10]{2,1,0:T(4,128)} reshape(f32[4,20480]{1,0:T(4,128)} %reduce.120) | data formatting | bytes 655360
  136.9 4.5 %copy.24 = f32[4,4,10,512]{3,1,0,2:T(4,128)} copy(f32[4,4,10,512]{2,1,3,0:T(4,128)} %bitcast.408) | data formatting | bytes 655360 | tf_op jit(solution)/shard_map/all_to_all | solution.py:65
  141.3 1.8 %all_to_all.16 = f32[16,10,512]{2,0,1:T(8,128)} reshape(f32[4,4,10,512]{3,1,0,2:T(4,128)} %copy.24) | data formatting | bytes 655360 | tf_op jit(solution)/shard_map/all_to_all | solution.py:65
  143.1 1.4 fusion.17
  144.6 1.1 copy.25
  (23 shorter events, 0.1 us)
Async XLA Ops:
  0.0 7.6 %copy-start = (bf16[4,10,80,512]{3,2,1,0:T(8,128)(2,1)S(1)}, bf16[4,10,80,512]{3,2,1,0:T(8,128)(2,1)}, u32[]{:S(2)}) copy-start(bf16[4,10,80,512]{3,2,1,0:T(8,128)(2,1)} %param.8) | copy-start | bytes 9830404
  13.3 17.5 %copy-start.2 = (bf16[1,5,16,12]{3,2,1,0:T(8,128)(2,1)S(1)}, bf16[1,5,16,12]{3,2,1,0:T(8,128)(2,1)}, u32[]{:S(2)}) copy-start(bf16[1,5,16,12]{3,2,1,0:T(8,128)(2,1)} %param.10) | copy-start | bytes 5764
  13.3 17.8 %copy-start.3 = (s32[1,5]{1,0:T(1,128)S(1)}, s32[1,5]{1,0:T(1,128)}, u32[]{:S(2)}) copy-start(s32[1,5]{1,0:T(1,128)} %param.11) | copy-start | bytes 64
  36.4 24.8 %copy-start.4 = (s32[1,5]{1,0:T(1,128)S(1)}, s32[1,5]{1,0:T(1,128)}, u32[]{:S(2)}) copy-start(s32[1,5]{1,0:T(1,128)} %param.13) | copy-start | bytes 64
  65.6 25.6 %collective-permute-start = (f32[81920]{0:T(1024)}, f32[81920]{0:T(1024)}, u32[]{:S(2)}, u32[]{:S(2)}) collective-permute-start(f32[81920]{0:T(1024)} %bitcast.90), channel_id=1, source_target_pairs={{2,0},{3,1},{4,2},{5,3},{6,4},{7,5},{10,8},{11,9},{12,10},{13,11},... | collective-permute-start | bytes 983048 | tf_op jit(solution)/shard_map/ppermute | solution.py:12
  73.0 18.2 %collective-permute-start.1 = (f32[81920]{0:T(1024)}, f32[81920]{0:T(1024)}, u32[]{:S(2)}, u32[]{:S(2)}) collective-permute-start(f32[81920]{0:T(1024)} %bitcast.93), channel_id=1, source_target_pairs={{1,0},{2,1},{3,2},{4,3},{5,4},{6,5},{7,6},{9,8},{10,9},{11,10},{12... | collective-permute-start | bytes 983048 | tf_op jit(solution)/shard_map/ppermute | solution.py:12
  79.9 13.5 %collective-permute-start.2 = (f32[81920]{0:T(1024)}, f32[81920]{0:T(1024)}, u32[]{:S(2)}, u32[]{:S(2)}) collective-permute-start(f32[81920]{0:T(1024)} %bitcast.96), channel_id=1, source_target_pairs={{0,1},{1,2},{2,3},{3,4},{4,5},{5,6},{6,7},{8,9},{9,10},{10,11},{11... | collective-permute-start | bytes 983048 | tf_op jit(solution)/shard_map/ppermute | solution.py:12
  83.9 5.0 %copy-start.1 = (f32[5,4,10,128,16]{3,4,2,1,0:T(8,128)S(1)}, f32[5,4,10,128,16]{3,4,2,1,0:T(8,128)}, u32[]{:S(2)}) copy-start(f32[5,4,10,128,16]{3,4,2,1,0:T(8,128)} %fusion) | copy-start | bytes 4915204
  87.6 10.5 %collective-permute-start.3 = (f32[81920]{0:T(1024)S(1)}, f32[81920]{0:T(1024)S(1)}, u32[]{:S(2)}, u32[]{:S(2)}) collective-permute-start(f32[81920]{0:T(1024)S(1)} %bitcast.410), channel_id=1, source_target_pairs={{0,2},{1,3},{2,4},{3,5},{4,6},{5,7},{8,10},{9,11},{10,12},{11,13},... | collective-permute-start | bytes 983048 | tf_op jit(solution)/shard_map/ppermute | solution.py:12
  106.4 11.4 %copy-start.5 = (f32[16,16]{1,0:T(8,128)S(1)}, f32[16,16]{1,0:T(8,128)}, u32[]{:S(2)}) copy-start(f32[16,16]{1,0:T(8,128)} %param.15) | copy-start | bytes 3076
  106.4 11.4 %copy-start.6 = (s32[16,1]{0,1:T(1,128)S(1)}, s32[16,1]{0,1:T(1,128)}, u32[]{:S(2)}) copy-start(s32[16,1]{0,1:T(1,128)} %param.14) | copy-start | bytes 196
  113.7 10.9 %all-to-all-start = ((f32[4,1,20480]{2,1,0:T(1,128)}), f32[4,1,20480]{2,1,0:T(1,128)}, u32[]{:S(2)}, u32[]{:S(2)}) async-start(f32[4,1,20480]{2,1,0:T(1,128)} %reshape.2638), calls=%async_computation | async-start | bytes 655360 | tf_op jit(solution)/shard_map/all_to_all | solution.py:65
where the time goes:
time: 147 us; the launch traced here: 146 us
  matrix products  51 us (35%)
  local copies, waits for them, and re-layouts  50.6 us (34%)
  other arithmetic  15.3 us (10%)
  starting transfers between devices  15 us (10%)
  waiting for transfers between devices  13.6 us (9%)
    dot_general x1, matrix products, body(): jnp.einsum('kir,dbrkj->kdbij', y_mats, x_pass, precision=lax.Precision.HI...  24.8 us
    dot_general x5, matrix products, aimed_at(): return jnp.dot(chosen, flat_parts, precision=lax.Precision.HIGHEST)  19 us
    reshape x1, local copies, waits for them, and re-layouts, body(): x_pass.reshape(local_dates, band_count, grid_rows, slot_count, tile_cols)  17.5 us
    unnamed x16, local copies, waits for them, and re-layouts  15.8 us
    ppermute x4, starting transfers between devices, shifted(): return lax.ppermute(block, axis, route)  10.9 us
    ppermute x4, waiting for transfers between devices, shifted(): return lax.ppermute(block, axis, route)  6.95 us
    unnamed x8, other arithmetic  6.89 us
    all_to_all x3, local copies, waits for them, and re-layouts, body(): lax.all_to_all(series, 'date', split_axis=2, concat_axis=0, tiled=True)  6.83 us
  transfers between devices with their start and end apart: 5, of which 3 were waited for; matrix products, arithmetic and copies ran while one was open for 10% of the time, Pallas kernels for 0%

commit v1 on v0

v1 whole, which is shorter than its diff:
```python
import functools

import jax
import jax.numpy as jnp
from jax import lax
from jax.experimental import pallas as pl
from jax.experimental.pallas import tpu as pltpu
from jax.sharding import PartitionSpec as P

RADIUS = 2
MESH = pl.DeviceIdType.MESH
ROWS = 64


def kernel(dims, tgt, roff, coff, mask, smoother, cx_ref, cy_ref, g_hbm, out_ref,
           g, rx, ymat, high, low, part, recv, final,
           g_sem, send1, recv1, send2, recv2):
    nt, nq, slots, tile_rows, tile_cols, taps, grid_rows, grid_cols, group, rpq, steps, all_dates, bands = dims
    reaches = list(range(-RADIUS, RADIUS + 1))
    home = RADIUS
    others = [0, 4, 1, 3]
    tile = lax.axis_index("tile")
    date = lax.axis_index("date")

    def fetch(step):
        return pltpu.make_async_copy(g_hbm.at[pl.ds(2 * step, 2)], g.at[pl.ds(2 * step, 2)], g_sem.at[step])

    for step in range(steps):
        fetch(step).start()

    def inside(place):
        return jnp.logical_and(place >= 0, place < nt)

    barrier = pltpu.get_barrier_semaphore()
    for ri in others:
        there = tile + reaches[ri]

        @pl.when(inside(there))
        def _(there=there):
            pl.semaphore_signal(barrier, inc=1, device_id=(date, there), device_id_type=MESH)

    for c in range(1, nq):
        pl.semaphore_signal(barrier, inc=1, device_id=(lax.rem(date + c, nq), tile), device_id_type=MESH)

    m_count, c_count = slots * tile_rows * group, group * grid_rows
    per_slot = tile_rows * group
    m_e = lax.broadcasted_iota(jnp.int32, (m_count, slots * tile_rows), 0)
    n_e = lax.broadcasted_iota(jnp.int32, (m_count, slots * tile_rows), 1)

    def row_of(m):
        return ((m % per_slot) // (group * rpq)) * rpq + m % rpq

    aimed = jnp.full_like(n_e, -1)
    for k in range(slots):
        aimed = jnp.where(n_e // tile_rows == k, tgt[0, k], aimed)
    wanted = m_e // per_slot + (tile - RADIUS)
    pick = jnp.where(jnp.logical_and(row_of(m_e) == n_e % tile_rows, aimed == wanted), 1.0, 0.0)
    cy = jnp.dot(pick.astype(jnp.bfloat16), cy_ref[...], preferred_element_type=jnp.float32)
    m = lax.broadcasted_iota(jnp.int32, (m_count, c_count), 0)
    c = lax.broadcasted_iota(jnp.int32, (m_count, c_count), 1)
    shift = jnp.zeros_like(m)
    reach_tile = m // per_slot + (tile - RADIUS)
    for k in range(slots):
        shift = jnp.where(reach_tile == tgt[0, k], roff[0, k], shift)
    band_c = jnp.zeros_like(c)
    for b in range(1, group):
        band_c = jnp.where(c >= b * grid_rows, b, band_c)
    tap = c - band_c * grid_rows - 2 * row_of(m) - shift
    tap = jnp.where((m // rpq) % group == band_c, tap, -1)
    acc = jnp.zeros((m_count, c_count), jnp.float32)
    for t in range(taps):
        acc = jnp.where(tap == t, cy[:, t:t + 1], acc)
    ymat[...] = acc.astype(jnp.bfloat16)

    def build(r, carry):
        want = tile + (r - RADIUS)
        coef = jnp.zeros((taps, tile_cols), jnp.float32)
        off = jnp.int32(0)
        for k in range(slots):
            hit = tgt[0, k] == want
            coef = coef + cx_ref[k].astype(jnp.float32) * jnp.where(hit, 1.0, 0.0)
            off = off + jnp.where(hit, coff[0, k], 0)
        row = lax.broadcasted_iota(jnp.int32, (ROWS, tile_cols), 0)
        lane = lax.broadcasted_iota(jnp.int32, (ROWS, tile_cols), 1)
        base = row - 2 * lane - off
        for j in range(grid_cols // ROWS):
            tap = base + j * ROWS
            acc = jnp.zeros((ROWS, tile_cols), jnp.float32)
            for t in range(taps):
                acc = jnp.where(tap == t, coef[t:t + 1, :], acc)
            rx[r, j * ROWS:(j + 1) * ROWS, :] = acc.astype(jnp.bfloat16)
        return carry

    lax.fori_loop(0, slots, build, 0)

    for step in range(steps):
        fetch(step).wait()
        pair = [
            jnp.dot(ymat[...], g[2 * step + h], preferred_element_type=jnp.float32).reshape(slots * nq, 1, 8, grid_cols)
            for h in range(2)
        ]
        both = jnp.concatenate(pair, 1).reshape(slots, nq, 16, grid_cols)
        top = both.astype(jnp.bfloat16)
        high[:, :, step * 16:(step + 1) * 16, :] = top
        low[:, :, step * 16:(step + 1) * 16, :] = (both - top.astype(jnp.float32)).astype(jnp.bfloat16)

    peers = jnp.int32(nq - 1)
    for ri in others:
        peers = peers + jnp.where(inside(tile + reaches[ri]), 1, 0)
    pl.semaphore_wait(barrier, peers)

    def to_tile(ri, q):
        return pltpu.make_async_remote_copy(
            src_ref=part.at[ri, q], dst_ref=recv.at[ri, q], send_sem=send1.at[ri, q], recv_sem=recv1.at[ri, q],
            device_id=(date, tile + reaches[ri]), device_id_type=MESH)

    def to_date(q):
        return pltpu.make_async_remote_copy(
            src_ref=part.at[home, q], dst_ref=final.at[date], send_sem=send2.at[q], recv_sem=recv2.at[date],
            device_id=(q, tile), device_id_type=MESH)

    def from_date(q):
        return pltpu.make_async_remote_copy(
            src_ref=part.at[home, q], dst_ref=final.at[q], send_sem=send2.at[q], recv_sem=recv2.at[q],
            device_id=(q, tile), device_id_type=MESH)

    order = [nq // 2] + [s for s in range(1, nq) if s != nq // 2] + [0]
    blocks = [lax.rem(date + s, nq) for s in order]
    for q in blocks:
        for ri in others + [home]:
            part[ri, q] = (
                jnp.dot(high[ri, q], rx[ri], preferred_element_type=jnp.float32)
                + jnp.dot(low[ri, q], rx[ri], preferred_element_type=jnp.float32))
            if ri != home:

                @pl.when(inside(tile + reaches[ri]))
                def _(ri=ri, q=q):
                    to_tile(ri, q).start()

    for s, q in zip(order, blocks):
        for ri in others:

            @pl.when(inside(tile - reaches[ri]))
            def _(ri=ri, q=q):
                to_tile(ri, q).wait_recv()
                part[home, q] = part[home, q] + recv[ri, q]

        if s != 0:
            to_date(q).start()
        else:
            final[date] = part[home, q]

    for s, q in zip(order, blocks):
        if s != 0:
            from_date(q).wait_recv()

    rows = bands * rpq
    here = all_dates // nq
    valid = [mask[0, s].astype(jnp.float32) for s in range(all_dates)]

    def smooth(t, carry):
        total = jnp.zeros((rows, tile_cols), jnp.float32)
        weight = jnp.float32(0.0)
        for s in range(all_dates):
            w = smoother[t, s] * valid[s]
            weight = weight + w
            first = (s % here) * rows
            total = total + final[s // here, first:first + rows, :] * w
        out_ref[t] = total / jnp.full((rows, tile_cols), weight, jnp.float32)
        return carry

    lax.fori_loop(0, all_dates, smooth, 0)

    for s, q in zip(order, blocks):
        for ri in others:

            @pl.when(inside(tile + reaches[ri]))
            def _(ri=ri, q=q):
                to_tile(ri, q).wait_send()

        if s != 0:
            to_date(q).wait_send()


def body(granules, coef_x, coef_y, row_offset, col_offset, targets, mask, smoother):
    dates, bands, grid_rows, grid_cols = granules.shape
    _, slots, tile_cols, taps = coef_x.shape
    tile_rows = coef_y.shape[2]
    nq, nt = lax.axis_size("date"), lax.axis_size("tile")
    rpq = tile_rows // nq
    group = 8 // rpq
    groups = dates * bands // group
    steps = groups // 2
    all_dates = smoother.shape[0]
    dims = (nt, nq, slots, tile_rows, tile_cols, taps, grid_rows, grid_cols, group, rpq, steps, all_dates, bands)
    block = dates * bands * rpq
    smem = pl.BlockSpec(memory_space=pltpu.SMEM)
    vmem = pl.BlockSpec(memory_space=pltpu.VMEM)
    dma = pltpu.SemaphoreType.DMA
    out = pl.pallas_call(
        functools.partial(kernel, dims),
        out_shape=jax.ShapeDtypeStruct((all_dates, bands * rpq, tile_cols), jnp.float32),
        in_specs=[smem] * 5 + [vmem, vmem, pl.BlockSpec(memory_space=pl.ANY)],
        out_specs=vmem,
        scratch_shapes=[
            pltpu.VMEM((groups, group * grid_rows, grid_cols), jnp.bfloat16),
            pltpu.VMEM((slots, grid_cols, tile_cols), jnp.bfloat16),
            pltpu.VMEM((slots * tile_rows * group, group * grid_rows), jnp.bfloat16),
            pltpu.VMEM((slots, nq, block, grid_cols), jnp.bfloat16),
            pltpu.VMEM((slots, nq, block, grid_cols), jnp.bfloat16),
            pltpu.VMEM((slots, nq, block, tile_cols), jnp.float32),
            pltpu.VMEM((slots, nq, block, tile_cols), jnp.float32),
            pltpu.VMEM((nq, block, tile_cols), jnp.float32),
            dma((steps,)),
            dma((slots, nq)),
            dma((slots, nq)),
            dma((nq,)),
            dma((nq,)),
        ],
        compiler_params=pltpu.CompilerParams(
            collective_id=0, has_side_effects=True, vmem_limit_bytes=48 * 1024 * 1024),
        cost_estimate=pl.CostEstimate(flops=2_000_000_000, bytes_accessed=4_000_000, transcendentals=0),
    )(targets, row_offset, col_offset, mask.reshape(1, all_dates), smoother,
      jnp.transpose(coef_x[0], (0, 2, 1)), coef_y[0].reshape(slots * tile_rows, taps),
      granules.reshape(groups, group * grid_rows, grid_cols))
    return out.reshape(all_dates, bands, 1, rpq * tile_cols)


def solution(mesh):
    return jax.shard_map(
        body,
        mesh=mesh,
        in_specs=(
            P("date", None, "tile", None),
            P("tile", None, None, None),
            P("tile", None, None, None),
            P("tile", None),
            P("tile", None),
            P("tile", None),
            P(None, "tile"),
            P(),
        ),
        out_specs=P(None, None, "tile", "date"),
        check_vma=False,
    )
```

time: 147 us -> 33.2 us (0.23)
  the two profiles are of different devices: /device:TPU:24 before, /device:TPU:17 now
where the time goes in v1:
time: 33.2 us; the launch traced here: 32.8 us
  Pallas kernels  25.4 us (77%)
  local copies, waits for them, and re-layouts  7.42 us (22%)
    pallas_call x1, Pallas kernels, body(): pl.pallas_call(functools.partial(kernel, dims), out_shape=jax.ShapeDtypeS...  25.4 us
    unnamed x17, local copies, waits for them, and re-layouts  7.42 us

profile of v1, /device:TPU:17, one launch (start us, length us, event | category | flops | bytes accessed | tf_op | source)
XLA Modules:
  0.0 32.8 jit_solution(6884992483796858102)
XLA Ops:
  0.0 0.0 copy-start
  0.0 1.9 %copy-done = bf16[4,10,80,512]{3,2,1,0:T(8,128)(2,1)S(1)} copy-done((bf16[4,10,80,512]{3,2,1,0:T(8,128)(2,1)S(1)}, bf16[4,10,80,512]{3,2,1,0:T(8,128)(2,1)}, u32[]{:S(2)}) %copy-start) | copy-done | bytes 3276824
  1.9 0.0 copy-start.1
  1.9 0.7 %copy-done.1 = bf16[1,5,128,12]{2,3,1,0:T(8,128)(2,1)S(1)} copy-done((bf16[1,5,128,12]{2,3,1,0:T(8,128)(2,1)S(1)}, bf16[1,5,128,12]{2,3,1,0:T(8,128)(2,1)}, u32[]{:S(2)}) %copy-start.1) | copy-done | bytes 15384
  2.7 0.0 copy-start.2
  2.7 0.7 %copy-done.2 = bf16[1,5,16,12]{3,2,1,0:T(8,128)(2,1)S(1)} copy-done((bf16[1,5,16,12]{3,2,1,0:T(8,128)(2,1)S(1)}, bf16[1,5,16,12]{3,2,1,0:T(8,128)(2,1)}, u32[]{:S(2)}) %copy-start.2) | copy-done | bytes 1944
  3.4 0.0 copy-start.3
  3.4 0.7 %copy-done.3 = f32[16,16]{1,0:T(8,128)S(1)} copy-done((f32[16,16]{1,0:T(8,128)S(1)}, f32[16,16]{1,0:T(8,128)}, u32[]{:S(2)}) %copy-start.3) | copy-done | bytes 1048
  4.1 0.0 copy-start.4
  4.1 0.7 %copy-done.4 = s32[1,5]{1,0:T(1,128)S(1)} copy-done((s32[1,5]{1,0:T(1,128)S(1)}, s32[1,5]{1,0:T(1,128)}, u32[]{:S(2)}) %copy-start.4) | copy-done | bytes 44
  4.7 0.0 copy-start.5
  4.7 0.7 %copy-done.5 = s32[1,5]{1,0:T(1,128)S(1)} copy-done((s32[1,5]{1,0:T(1,128)S(1)}, s32[1,5]{1,0:T(1,128)}, u32[]{:S(2)}) %copy-start.5) | copy-done | bytes 44
  5.4 0.0 copy-start.6
  5.4 0.7 %copy-done.6 = s32[1,5]{1,0:T(1,128)S(1)} copy-done((s32[1,5]{1,0:T(1,128)S(1)}, s32[1,5]{1,0:T(1,128)}, u32[]{:S(2)}) %copy-start.6) | copy-done | bytes 44
  6.0 0.0 copy-start.7
  6.0 0.7 %copy-done.7 = s32[16,1]{0,1:T(1,128)S(1)} copy-done((s32[16,1]{0,1:T(1,128)S(1)}, s32[16,1]{0,1:T(1,128)}, u32[]{:S(2)}) %copy-start.7) | copy-done | bytes 88
  6.7 25.4 %shard_map.82 = f32[16,40,128]{2,1,0:T(8,128)S(1)} custom-call(s32[1,5]{1,0:T(1,128)S(1)} %copy-done.4, s32[1,5]{1,0:T(1,128)S(1)} %copy-done.5, s32[1,5]{1,0:T(1,128)S(1)} %copy-done.6, s32[1,16]{1,0:T(1,128)S(1)} %bitcast.11, f32[16,16]{1,0:T(8,128)S(1)} %copy-done.3, bf16[5,12,128]{2,1,0:T(8,128)(2,1)S(1)} %bitcast.9, bf16[80,12]{1,0:T(8,128)(2,1)S(1)} %bitcast.10, ...), custom_call_target="tpu_custom_call" | custom-call | flops 2000000000 | bytes 4000000 | tf_op jit(solution)/shard_map/pallas_call | solution.py:200
  32.1 0.7 %copy.12 = f32[16,10,1,512]{3,2,1,0:T(1,128)} copy(f32[16,10,1,512]{3,2,1,0:T(1,128)S(1)} %bitcast.7) | data formatting | bytes 655360
Async XLA Ops:
  0.0 1.9 %copy-start = (bf16[4,10,80,512]{3,2,1,0:T(8,128)(2,1)S(1)}, bf16[4,10,80,512]{3,2,1,0:T(8,128)(2,1)}, u32[]{:S(2)}) copy-start(bf16[4,10,80,512]{3,2,1,0:T(8,128)(2,1)} %param.8) | copy-start | bytes 9830404
  1.9 0.7 %copy-start.1 = (bf16[1,5,128,12]{2,3,1,0:T(8,128)(2,1)S(1)}, bf16[1,5,128,12]{2,3,1,0:T(8,128)(2,1)}, u32[]{:S(2)}) copy-start(bf16[1,5,128,12]{2,3,1,0:T(8,128)(2,1)} %param.9) | copy-start | bytes 46084
  2.7 0.7 %copy-start.2 = (bf16[1,5,16,12]{3,2,1,0:T(8,128)(2,1)S(1)}, bf16[1,5,16,12]{3,2,1,0:T(8,128)(2,1)}, u32[]{:S(2)}) copy-start(bf16[1,5,16,12]{3,2,1,0:T(8,128)(2,1)} %param.10) | copy-start | bytes 5764
  3.4 0.7 %copy-start.3 = (f32[16,16]{1,0:T(8,128)S(1)}, f32[16,16]{1,0:T(8,128)}, u32[]{:S(2)}) copy-start(f32[16,16]{1,0:T(8,128)} %smoother.1) | copy-start | bytes 3076
  4.1 0.7 %copy-start.4 = (s32[1,5]{1,0:T(1,128)S(1)}, s32[1,5]{1,0:T(1,128)}, u32[]{:S(2)}) copy-start(s32[1,5]{1,0:T(1,128)} %tgt.1) | copy-start | bytes 64
  4.7 0.7 %copy-start.5 = (s32[1,5]{1,0:T(1,128)S(1)}, s32[1,5]{1,0:T(1,128)}, u32[]{:S(2)}) copy-start(s32[1,5]{1,0:T(1,128)} %roff.1) | copy-start | bytes 64
  5.4 0.7 %copy-start.6 = (s32[1,5]{1,0:T(1,128)S(1)}, s32[1,5]{1,0:T(1,128)}, u32[]{:S(2)}) copy-start(s32[1,5]{1,0:T(1,128)} %coff.1) | copy-start | bytes 64
  6.0 0.7 %copy-start.7 = (s32[16,1]{0,1:T(1,128)S(1)}, s32[16,1]{0,1:T(1,128)}, u32[]{:S(2)}) copy-start(s32[16,1]{0,1:T(1,128)} %param.14) | copy-start | bytes 196
